TPU v7x, 32 devices: a whole 2x2x4 slice. The times are simulated.
32 devices in a mesh: dp: 8 (over y, x, core), tensor: 4 (over z).
Axes of the slice: x: 2, y: 2, z: 4, core: 2. Of those that a mesh axis runs over, the one named last changes fastest.
Arguments:
- inputs: bfloat16 [2048, 1024], P(('dp', 'tensor')), may hold values from -6 to 6
- first_gain: float32 [1024], replicated, may hold values from 0.1 to 1.9
- entry_projection_weight: bfloat16 [3, 1024, 1024], P(None, 'dp', 'tensor'), may hold values from -0.1875 to 0.1875
- conv_weight: float32 [3, 1024], replicated, may hold values from -3 to 3
- out_weight: bfloat16 [1024, 1024], P('tensor', 'dp'), may hold values from -0.1875 to 0.1875
- second_gain: float32 [1024], replicated, may hold values from 0.1 to 1.9
- gate_up_weight: bfloat16 [2, 1024, 4608], P(None, 'dp', 'tensor'), may hold values from -0.1875 to 0.1875
- down_weight: bfloat16 [4608, 1024], P('tensor', 'dp'), may hold values from -0.09375 to 0.09375
- cotangent: bfloat16 [2048, 1024], P(('dp', 'tensor')), may hold values from -6 to 6
- lengths: int32 [4], replicated, may hold values from 1 to 1024, 2048 in all
Outputs:
- output: bfloat16 [2048, 1024], P(('dp', 'tensor'))
- input_grad: float32 [2048, 1024], P(('dp', 'tensor'))
- first_gain_grad: float32 [1024], replicated
- in_weight_grad: float32 [3, 1024, 1024], P(None, 'dp', 'tensor')
- filter_weight_gradient: float32 [3, 1024], replicated
- out_weight_grad: float32 [1024, 1024], P('tensor', 'dp')
- second_gain_grad: float32 [1024], replicated
- gate_up_grad: float32 [2, 1024, 4608], P(None, 'dp', 'tensor')
- down_grad: float32 [4608, 1024], P('tensor', 'dp')
Inputs may be any that keep to these rules, and one draw needn't show every extreme that they name: lengths of the 4 sequences packed end to end in token order; they sum to 2048, and the longest is exactly 1024.
All inputs are finite; a program needn't handle non-finite values.
Results may differ from a plain program's by a relative error of at most 0.012.
Values may be sent and summed in bfloat16 or wider, within the bound.
A program may use at most 128 MiB of HBM per device.

v0:
```python
import jax
import jax.numpy as jnp
from jax import lax
from jax.sharding import PartitionSpec as P

EPS = 1e-05


def passed_along(block, axis, distance):
    devices = range(lax.axis_size(axis))
    route = [(i - distance, i) for i in devices if i - distance in devices]
    return lax.ppermute(block, axis, route)


def rms_norm(values, gain):
    return values * lax.rsqrt(jnp.mean(values * values, axis=-1, keepdims=True) + EPS) * gain


def rms_back(values, gain, grad_out):
    scale = lax.rsqrt(jnp.mean(values * values, axis=-1, keepdims=True) + EPS)
    normal = values * scale
    weighted = gain * grad_out
    grad_in = scale * (weighted - normal * jnp.mean(normal * weighted, axis=-1, keepdims=True))
    return (grad_in, jnp.sum(normal * grad_out, axis=0))


def times_trans(left, right):
    return lax.dot_general(
        left, right, (((1,), (1,)), ((), ())), preferred_element_type=jnp.float32
    )


def trans_times(left, right):
    return lax.dot_general(
        left, right, (((0,), (0,)), ((), ())), preferred_element_type=jnp.float32
    )


def shards(
    inputs,
    first_gain,
    entry_projection_weight,
    conv_weight,
    out_weight,
    second_gain,
    gate_up_weight,
    down_weight,
    cotangent,
    lengths,
):
    own_rows = inputs.shape[0]
    group_rows = own_rows * lax.axis_size("tensor")
    channels = entry_projection_weight.shape[2]
    column = lax.axis_index("tensor") * channels
    start = lax.axis_index("dp") * group_rows
    ends = jnp.cumsum(lengths)
    places = start - 2 + jnp.arange(group_rows + 4, dtype=jnp.int32)
    segment = jnp.sum((places[:, None] >= ends[None, :]).astype(jnp.int32), axis=1)
    first_all = jnp.logical_and(segment[2:] == segment[1:-1], places[2:] >= 1).astype(jnp.float32)[
        :, None
    ]
    second_all = jnp.logical_and(segment[2:] == segment[:-2], places[2:] >= 2).astype(jnp.float32)[
        :, None
    ]
    first_keep = first_all[:group_rows]
    second_keep = second_all[:group_rows]
    kernel = lax.dynamic_slice_in_dim(conv_weight, column, channels, 1)
    residual = inputs.astype(jnp.float32)
    normed = lax.all_gather(
        rms_norm(residual, first_gain).astype(jnp.bfloat16), "tensor", axis=0, tiled=True
    )
    in_full, out_full, gate_up_full, down_full = (
        lax.all_gather(entry_projection_weight, "dp", axis=1, tiled=True),
        lax.all_gather(out_weight, "dp", axis=1, tiled=True),
        lax.all_gather(gate_up_weight, "dp", axis=1, tiled=True),
        lax.all_gather(down_weight, "dp", axis=1, tiled=True),
    )
    projected = jnp.einsum("td,kdc->ktc", normed, in_full, preferred_element_type=jnp.float32)
    input_gate_value = projected[0]
    c_value = projected[1]
    v_value = projected[2]
    product = (input_gate_value * v_value).astype(jnp.bfloat16)
    before = passed_along(product[-2:], "dp", 1)
    extended = jnp.concatenate([before, product], axis=0).astype(jnp.float32)
    mixed = (
        kernel[2] * extended[2:]
        + kernel[1] * first_keep * extended[1:-1]
        + kernel[0] * second_keep * extended[:-2]
    )
    gated = (c_value * mixed).astype(jnp.bfloat16)
    mixer_part = jnp.dot(gated, out_full, preferred_element_type=jnp.float32)
    middle = residual + lax.psum_scatter(mixer_part, "tensor", scatter_dimension=0, tiled=True)
    hidden_in = lax.all_gather(
        rms_norm(middle, second_gain).astype(jnp.bfloat16), "tensor", axis=0, tiled=True
    )
    gate_up = jnp.einsum("td,kdf->ktf", hidden_in, gate_up_full, preferred_element_type=jnp.float32)
    gate_value = gate_up[0]
    up_value = gate_up[1]
    sigmoid = jax.nn.sigmoid(gate_value)
    swish = gate_value * sigmoid
    hidden = (swish * up_value).astype(jnp.bfloat16)
    ffn_part = jnp.dot(hidden, down_full, preferred_element_type=jnp.float32)
    output = (
        middle
        + lax.psum_scatter(
            ffn_part.astype(jnp.bfloat16), "tensor", scatter_dimension=0, tiled=True
        ).astype(jnp.float32)
    ).astype(jnp.bfloat16)
    in_full, out_full, gate_up_full, down_full = (
        lax.all_gather(entry_projection_weight, "dp", axis=1, tiled=True),
        lax.all_gather(out_weight, "dp", axis=1, tiled=True),
        lax.all_gather(gate_up_weight, "dp", axis=1, tiled=True),
        lax.all_gather(down_weight, "dp", axis=1, tiled=True),
    )
    grad_rows = lax.all_gather(cotangent, "tensor", axis=0, tiled=True)
    grad_hidden = times_trans(grad_rows, down_full)
    down_part = trans_times(hidden, grad_rows)
    grad_gate = (grad_hidden * up_value * sigmoid * (1.0 + gate_value * (1.0 - sigmoid))).astype(
        jnp.bfloat16
    )
    grad_up = (grad_hidden * swish).astype(jnp.bfloat16)
    gate_up_stack = jnp.stack([grad_gate, grad_up])
    gate_up_part = jnp.einsum(
        "td,ktf->kdf", hidden_in, gate_up_stack, preferred_element_type=jnp.float32
    )
    hidden_back = jnp.einsum(
        "ktf,kdf->td", gate_up_stack, gate_up_full, preferred_element_type=jnp.float32
    )
    grad_hin = lax.psum_scatter(hidden_back, "tensor", scatter_dimension=0, tiled=True)
    second_back, second_part = rms_back(middle, second_gain, grad_hin)
    grad_middle = cotangent.astype(jnp.float32) + second_back
    branch_rows = lax.all_gather(grad_middle.astype(jnp.bfloat16), "tensor", axis=0, tiled=True)
    grad_gated = times_trans(branch_rows, out_full)
    out_part = trans_times(gated, branch_rows)
    output_gate_gradient = (grad_gated * mixed).astype(jnp.bfloat16)
    grad_mixed = (grad_gated * c_value).astype(jnp.bfloat16)
    after = passed_along(grad_mixed[:2], "dp", -1)
    grad_ext = jnp.concatenate([grad_mixed, after], axis=0).astype(jnp.float32)
    mixed_wide = grad_ext[:-2]
    kernel_part = jnp.stack(
        [
            jnp.sum(second_keep * extended[:-2] * mixed_wide, axis=0),
            jnp.sum(first_keep * extended[1:-1] * mixed_wide, axis=0),
            jnp.sum(extended[2:] * mixed_wide, axis=0),
        ]
    )
    kernel_full = lax.dynamic_update_slice_in_dim(
        jnp.zeros(conv_weight.shape, jnp.float32), kernel_part, column, 1
    )
    elementwise_product_gradient = (
        kernel[2] * grad_ext[:-2]
        + kernel[1] * first_all[1:-1] * grad_ext[1:-1]
        + kernel[0] * second_all[2:] * grad_ext[2:]
    )
    input_gate_gradient = (elementwise_product_gradient * v_value).astype(jnp.bfloat16)
    value_branch_gradient = (elementwise_product_gradient * input_gate_value).astype(jnp.bfloat16)
    stacked_projection_outputs = jnp.stack(
        [input_gate_gradient, output_gate_gradient, value_branch_gradient]
    )
    in_part = jnp.einsum(
        "td,ktc->kdc", normed, stacked_projection_outputs, preferred_element_type=jnp.float32
    )
    normed_back = jnp.einsum(
        "ktc,kdc->td", stacked_projection_outputs, in_full, preferred_element_type=jnp.float32
    )
    grad_normed = lax.psum_scatter(
        normed_back.astype(jnp.bfloat16), "tensor", scatter_dimension=0, tiled=True
    ).astype(jnp.float32)
    first_back, first_part = rms_back(residual, first_gain, grad_normed)
    input_grad = grad_middle + first_back
    in_grad, out_grad, gate_up_grad, down_grad = (
        lax.psum_scatter(in_part, "dp", scatter_dimension=1, tiled=True),
        lax.psum_scatter(out_part, "dp", scatter_dimension=1, tiled=True),
        lax.psum_scatter(gate_up_part, "dp", scatter_dimension=1, tiled=True),
        lax.psum_scatter(down_part, "dp", scatter_dimension=1, tiled=True),
    )
    first_gain_grad, second_gain_grad, conv_grad = lax.psum(
        (first_part, second_part, kernel_full), ("dp", "tensor")
    )
    return (
        output,
        input_grad,
        first_gain_grad,
        in_grad,
        conv_grad,
        out_grad,
        second_gain_grad,
        gate_up_grad,
        down_grad,
    )


def solution(mesh):
    in_specs = (
        P(("dp", "tensor"), None),
        P(),
        P(None, "dp", "tensor"),
        P(),
        P("tensor", "dp"),
        P(),
        P(None, "dp", "tensor"),
        P("tensor", "dp"),
        P(("dp", "tensor"), None),
        P(),
    )
    out_specs = (
        P(("dp", "tensor"), None),
        P(("dp", "tensor"), None),
        P(),
        P(None, "dp", "tensor"),
        P(),
        P("tensor", "dp"),
        P(),
        P(None, "dp", "tensor"),
        P("tensor", "dp"),
    )
    return jax.shard_map(shards, mesh=mesh, in_specs=in_specs, out_specs=out_specs, check_vma=False)
```

profile of v0, /device:TPU:0, one launch (start us, length us, event | category | flops | bytes accessed | tf_op | source)
XLA Modules:
  0.0 489.5 jit_solution(4341568830876603250)
XLA Ops:
  7.2 0.7 all-gather.4.cloned.1.call-update
  8.0 0.8 reduce-window.8
  8.9 11.7 %all_gather.30 = bf16[256,1024]{1,0:T(8,128)(2,1)S(1)} all-gather(bf16[256,128]{1,0:T(8,128)(2,1)} %param.14), channel_id=1, replica_groups=mesh['dp'=8,'tensor'=4] {'dp'}, dimensions={1}, use_global_device_ids=true | all-gather | bytes 589824 | tf_op jit(solution)/shard_map/all_gather | solution.py:74
  20.6 1.1 fusion.18
  21.8 1.0 fusion.15
  22.8 16.4 %all_gather.28 = bf16[256,1024]{1,0:T(8,128)(2,1)S(1)} all-gather(bf16[64,1024]{1,0:T(8,128)(2,1)S(1)} %fusion.15), channel_id=1, replica_groups=mesh['dp'=8,'tensor'=4] {'tensor'}, dimensions={0}, use_global_device_ids=true | all-gather | bytes 655360 | tf_op jit(solution)/shard_map/all_gather | solution.py:69
  39.3 0.7 fusion.35
  39.9 2.0 convolution_bitcast_fusion.5
  42.0 1.3 collective-permute-start
  43.3 0.9 fusion.34
  44.2 0.9 multiply_convert_fusion.8
  45.1 1.3 fusion.37
  46.5 0.7 all-gather.6.cloned.1.call-update
  47.8 21.5 %all_gather.34 = bf16[256,1024]{1,0:T(8,128)(2,1)} all-gather(bf16[64,1024]{1,0:T(8,128)(2,1)S(1)} %copy-done.13), channel_id=1, replica_groups=mesh['dp'=8,'tensor'=4] {'tensor'}, dimensions={0}, use_global_device_ids=true | all-gather | bytes 655360 | tf_op jit(solution)/shard_map/all_gather | solution.py:115
  69.3 13.1 %reduce-scatter.9.cloned.1.call-done = f32[64,1024]{1,0:T(8,128)} async-done(((f32[256,1024]{1,0:T(8,128)}), f32[64,1024]{1,0:T(8,128)}) %reduce-scatter.9.cloned.1.call-update) | async-done | bytes 262160 | tf_op jit(solution)/shard_map/reduce_scatter | solution.py:92
  82.4 1.1 multiply_reduce_fusion.5
  83.6 16.7 %all_gather.31 = bf16[256,1024]{1,0:T(8,128)(2,1)} all-gather(bf16[64,1024]{1,0:T(8,128)(2,1)S(1)} %multiply_convert_fusion.7), channel_id=1, replica_groups=mesh['dp'=8,'tensor'=4] {'tensor'}, dimensions={0}, use_global_device_ids=true | all-gather | bytes 655360 | tf_op jit(solution)/shard_map/all_gather | solution.py:93
  100.3 22.1 %all-gather.6.cloned.1.call-done = bf16[2,1024,1152]{2,1,0:T(8,128)(2,1)} async-done(((bf16[2,128,1152]{2,1,0:T(8,128)(2,1)}), bf16[2,1024,1152]{2,1,0:T(8,128)(2,1)}) %all-gather.6.cloned.1.call-update) | async-done | bytes 4718608 | tf_op jit(solution)/shard_map/all_gather | solution.py:75
  122.4 3.9 convolution_bitcast_fusion.1
  126.2 27.4 %all-gather.8.cloned.1.call-done = bf16[1152,1024]{1,0:T(8,128)(2,1)} async-done(((bf16[1152,128]{1,0:T(8,128)(2,1)}), bf16[1152,1024]{1,0:T(8,128)(2,1)}) %all-gather.8.cloned.1.call-update) | async-done | bytes 2359312 | tf_op jit(solution)/shard_map/all_gather | solution.py:76
  153.6 4.1 fusion.3
  157.7 0.8 copy-done.18
  158.7 2.4 convolution_bitcast_fusion.4
  161.2 27.2 %reduce-scatter.13.cloned.1.call-done = f32[64,1024]{1,0:T(8,128)} async-done(((f32[256,1024]{1,0:T(8,128)}), f32[64,1024]{1,0:T(8,128)}) %reduce-scatter.13.cloned.1.call-update) | async-done | bytes 262160 | tf_op jit(solution)/shard_map/reduce_scatter | solution.py:129
  188.4 1.2 multiply_reduce_fusion
  190.1 1.1 fusion.32
  191.3 15.9 %all_gather.35 = bf16[256,1024]{1,0:T(8,128)(2,1)S(1)} all-gather(bf16[64,1024]{1,0:T(8,128)(2,1)S(1)} %fusion.32), channel_id=1, replica_groups=mesh['dp'=8,'tensor'=4] {'tensor'}, dimensions={0}, use_global_device_ids=true | all-gather | bytes 655360 | tf_op jit(solution)/shard_map/all_gather | solution.py:132
  207.7 1.4 collective-permute-start.1
  209.1 1.7 collective-permute-done.1
  210.9 0.8 multiply_reduce_fusion.3
  211.8 1.4 fusion
  213.4 3.4 convolution_convert_fusion
  216.9 2.3 convolution_bitcast_fusion.2
  219.2 1.0 copy-done.3
  220.4 6.2 %convolution_bitcast_fusion = f32[2,1024,1152]{1,2,0:T(8,128)} fusion(bf16[1,256,1152]{2,1,0:T(8,128)(2,1)} %copy-done.20, bf16[1,256,1152]{2,1,0:T(8,128)(2,1)S(1)} %copy-done.19, bf16[256,1024]{1,0:T(8,128)(2,1)S(1)} %copy-done.3), kind=kOutput, calls=%fused_computation | convolution fusion | flops 1208549376 | bytes 11141120 | tf_op jit(solution)/shard_map/td,ktf->kdf/dot_general | solution.py:123
  226.6 0.8 copy-done.16
  227.4 1.3 fusion.39
  228.8 3.0 fusion.40
  232.6 1.5 reduce-scatter.15.cloned.1.call-done
  234.1 1.1 fusion.17
  235.2 39.3 %all-reduce = (f32[1024]{0:T(1024)}, f32[3,1024]{1,0:T(4,128)}, f32[1024]{0:T(1024)}) all-reduce(f32[1024]{0:T(1024)S(1)} %get-tuple-element.32, f32[3,1024]{1,0:T(4,128)S(1)} %maximum_dynamic-update-slice_fusion, f32[1024]{0:T(1024)S(1)} %get-tuple-element.30), channel_id=1, replica_groups=mesh['dp'=8,'tensor'=4] {'dp','tensor'}, use_global_device_ids=true, to_apply=%region_11.12 | all-reduce | flops 5120 | bytes 40960 | tf_op jit(solution)/shard_map/psum | solution.py:177
  274.6 1.9 fusion.14
  276.5 27.7 %reduce-scatter.17.cloned.1.call-done = f32[3,128,256]{1,2,0:T(8,128)} async-done(((f32[3,1024,256]{1,2,0:T(8,128)}), f32[3,128,256]{1,2,0:T(8,128)}) %reduce-scatter.17.cloned.1.call-update) | async-done | bytes 393232 | tf_op jit(solution)/shard_map/reduce_scatter | solution.py:172
  304.2 1.9 copy.25
  306.1 78.5 %reduce-scatter.21.cloned.1.call-done = f32[2,128,1152]{1,2,0:T(8,128)} async-done(((f32[2,1024,1152]{1,2,0:T(8,128)}), f32[2,128,1152]{1,2,0:T(8,128)}) %reduce-scatter.21.cloned.1.call-update) | async-done | bytes 1179664 | tf_op jit(solution)/shard_map/reduce_scatter | solution.py:174
  384.6 2.7 copy.26
  387.3 37.3 %reduce-scatter.19.cloned.1.call-done = f32[256,128]{1,0:T(8,128)} async-done(((f32[256,1024]{1,0:T(8,128)}), f32[256,128]{1,0:T(8,128)}) %reduce-scatter.19.cloned.1.call-update) | async-done | bytes 131088 | tf_op jit(solution)/shard_map/reduce_scatter | solution.py:173
  424.6 58.3 %reduce-scatter.23.cloned.1.call-done = f32[1152,128]{1,0:T(8,128)} async-done(((f32[1152,1024]{1,0:T(8,128)}), f32[1152,128]{1,0:T(8,128)}) %reduce-scatter.23.cloned.1.call-update) | async-done | bytes 589840 | tf_op jit(solution)/shard_map/reduce_scatter | solution.py:175
  (136 shorter events, 3.6 us)
Async XLA Ops:
  7.2 32.7 %all-gather.4.cloned.1.call-start = ((), (), s32[]{:S(2)}) async-start(), calls=%async_computation.8 | async-start | bytes 1769472 | tf_op jit(solution)/shard_map/all_gather | solution.py:73
  7.9 74.5 %reduce-scatter.9.cloned.1.call-start = ((), (), s32[]{:S(2)}) async-start(), calls=%async_computation.9 | async-start | bytes 1310720 | tf_op jit(solution)/shard_map/reduce_scatter | solution.py:92
  20.6 24.5 %copy-start.4 = (bf16[256,1024]{1,0:T(8,128)(2,1)}, bf16[256,1024]{1,0:T(8,128)(2,1)S(1)}, u32[]{:S(2)}) copy-start(bf16[256,1024]{1,0:T(8,128)(2,1)S(1)} %all_gather.30) | copy-start | bytes 1572868
  21.8 17.5 %copy-start.40 = (f32[64]{0:T(128)}, f32[64]{0:T(128)S(1)}, u32[]{:S(2)}) copy-start(f32[64]{0:T(128)S(1)} %add_rsqrt_fusion.1) | copy-start | bytes 772
  39.2 2.8 copy-start.6
  39.9 4.3 copy-start.33
  39.9 4.3 copy-start.35
  42.0 2.2 collective-permute-start
  45.1 2.1 copy-start.15
  45.1 2.7 copy-start.13
  46.4 36.0 %copy-start.8 = (bf16[64,1024]{1,0:T(8,128)(2,1)S(1)}, bf16[64,1024]{1,0:T(8,128)(2,1)}, u32[]{:S(2)}) copy-start(bf16[64,1024]{1,0:T(8,128)(2,1)} %param.10) | copy-start | bytes 393220
  46.4 37.1 %copy-start.25 = (f32[1024]{0:T(1024)S(1)}, f32[1024]{0:T(1024)}, u32[]{:S(2)}) copy-start(f32[1024]{0:T(1024)} %param.15) | copy-start | bytes 12292
  46.4 75.9 %all-gather.6.cloned.1.call-start = ((), (), s32[]{:S(2)}) async-start(), calls=%async_computation.10 | async-start | bytes 5308416 | tf_op jit(solution)/shard_map/all_gather | solution.py:75
  47.2 106.4 %all-gather.8.cloned.1.call-start = ((), (), s32[]{:S(2)}) async-start(), calls=%async_computation.11 | async-start | bytes 2654208 | tf_op jit(solution)/shard_map/all_gather | solution.py:76
  47.8 140.6 %reduce-scatter.13.cloned.1.call-start = ((), (), s32[]{:S(2)}) async-start(), calls=%async_computation.13 | async-start | bytes 1310720 | tf_op jit(solution)/shard_map/reduce_scatter | solution.py:129
  83.5 16.8 %copy-start.1 = (f32[64,1024]{1,0:T(8,128)}, f32[64,1024]{1,0:T(8,128)S(1)}, u32[]{:S(2)}) copy-start(f32[64,1024]{1,0:T(8,128)S(1)} %get-tuple-element.40) | copy-start | bytes 786436
  83.5 16.8 %copy-start.37 = (f32[64]{0:T(128)}, f32[64]{0:T(128)S(1)}, u32[]{:S(2)}) copy-start(f32[64]{0:T(128)S(1)} %add_rsqrt_fusion) | copy-start | bytes 772
  153.6 5.1 %copy-start = (bf16[2,1024,1152]{2,1,0:T(8,128)(2,1)S(1)}, bf16[2,1024,1152]{2,1,0:T(8,128)(2,1)}, u32[]{:S(2)}) copy-start(bf16[2,1024,1152]{2,1,0:T(8,128)(2,1)} %all-gather.6.cloned.1.call-done) | copy-start | bytes 14155780
  158.7 29.7 %copy-start.2 = (f32[64,1024]{1,0:T(8,128)S(1)}, f32[64,1024]{1,0:T(8,128)}, u32[]{:S(2)}) copy-start(f32[64,1024]{1,0:T(8,128)} %copy-done.1) | copy-start | bytes 786436
  158.7 29.7 %copy-start.38 = (f32[64]{0:T(128)S(1)}, f32[64]{0:T(128)}, u32[]{:S(2)}) copy-start(f32[64]{0:T(128)} %copy-done.37) | copy-start | bytes 772
  161.1 29.0 %copy-start.14 = (bf16[64,1024]{1,0:T(8,128)(2,1)S(1)}, bf16[64,1024]{1,0:T(8,128)(2,1)}, u32[]{:S(2)}) copy-start(bf16[64,1024]{1,0:T(8,128)(2,1)} %param.18) | copy-start | bytes 393220
  161.1 46.1 %copy-start.5 = (bf16[256,1024]{1,0:T(8,128)(2,1)S(1)}, bf16[256,1024]{1,0:T(8,128)(2,1)}, u32[]{:S(2)}) copy-start(bf16[256,1024]{1,0:T(8,128)(2,1)} %copy-done.4) | copy-start | bytes 1572868
  161.1 46.4 %copy-start.17 = (f32[256,256]{1,0:T(8,128)S(1)}, f32[256,256]{1,0:T(8,128)}, u32[]{:S(2)}) copy-start(f32[256,256]{1,0:T(8,128)} %get-tuple-element.42) | copy-start | bytes 786436
  161.1 73.0 %reduce-scatter.15.cloned.1.call-start = ((), (), s32[]{:S(2)}) async-start(), calls=%async_computation.14 | async-start | bytes 655360 | tf_op jit(solution)/shard_map/reduce_scatter | solution.py:166
  191.2 19.6 %copy-start.28 = (f32[1,256]{1,0:T(1,128)S(1)}, f32[1,256]{1,0:T(1,128)}, u32[]{:S(2)}) copy-start(f32[1,256]{1,0:T(1,128)} %copy-done.27) | copy-start | bytes 3076
  191.2 19.6 %copy-start.30 = (f32[1,256]{1,0:T(1,128)S(1)}, f32[1,256]{1,0:T(1,128)}, u32[]{:S(2)}) copy-start(f32[1,256]{1,0:T(1,128)} %copy-done.29) | copy-start | bytes 3076
  191.2 19.6 %copy-start.32 = (f32[1,256]{1,0:T(1,128)S(1)}, f32[1,256]{1,0:T(1,128)}, u32[]{:S(2)}) copy-start(f32[1,256]{1,0:T(1,128)} %copy-done.31) | copy-start | bytes 3076
  191.2 19.6 %copy-start.34 = (f32[256]{0:T(256)S(1)}, f32[256]{0:T(256)}, u32[]{:S(2)}) copy-start(f32[256]{0:T(256)} %copy-done.33) | copy-start | bytes 3076
  191.2 19.6 %copy-start.36 = (f32[256]{0:T(256)S(1)}, f32[256]{0:T(256)}, u32[]{:S(2)}) copy-start(f32[256]{0:T(256)} %copy-done.35) | copy-start | bytes 3076
  191.3 19.6 %copy-start.45 = (f32[256]{0:T(256)S(1)}, f32[256]{0:T(256)}, u32[]{:S(2)}) copy-start(f32[256]{0:T(256)} %get-tuple-element.57) | copy-start | bytes 3076
  191.3 19.6 %copy-start.46 = (f32[256]{0:T(256)S(1)}, f32[256]{0:T(256)}, u32[]{:S(2)}) copy-start(f32[256]{0:T(256)} %get-tuple-element.62) | copy-start | bytes 3076
  207.6 4.2 copy-start.23
  207.7 4.2 copy-start.11
  207.7 3.2 collective-permute-start.1
  213.3 61.3 %reduce-scatter.11.cloned.1.call-start = ((), (), s32[]{:S(2)}) async-start(), calls=%async_computation.12 | async-start | bytes 655360 | tf_op jit(solution)/shard_map/reduce_scatter | solution.py:105
  213.3 3.5 copy-start.7
  213.3 3.5 copy-start.22
  213.4 3.5 copy-start.24
  216.8 87.4 %reduce-scatter.17.cloned.1.call-start = ((), (), s32[]{:S(2)}) async-start(), calls=%async_computation.15 | async-start | bytes 3538944 | tf_op jit(solution)/shard_map/reduce_scatter | solution.py:172
  219.2 165.5 %reduce-scatter.21.cloned.1.call-start = ((), (), s32[]{:S(2)}) async-start(), calls=%async_computation.17 | async-start | bytes 10616832 | tf_op jit(solution)/shard_map/reduce_scatter | solution.py:174
  226.6 2.3 copy-start.10
  226.6 198.1 %reduce-scatter.19.cloned.1.call-start = ((), (), s32[]{:S(2)}) async-start(), calls=%async_computation.16 | async-start | bytes 1179648 | tf_op jit(solution)/shard_map/reduce_scatter | solution.py:173
  228.8 254.2 %reduce-scatter.23.cloned.1.call-start = ((), (), s32[]{:S(2)}) async-start(), calls=%async_computation.18 | async-start | bytes 5308416 | tf_op jit(solution)/shard_map/reduce_scatter | solution.py:175
  231.9 2.2 copy-start.26
  231.9 2.2 copy-start.41
  231.9 42.7 %copy-start.9 = (f32[64,1024]{1,0:T(8,128)S(1)}, f32[64,1024]{1,0:T(8,128)}, u32[]{:S(2)}) copy-start(f32[64,1024]{1,0:T(8,128)} %reduce-scatter.13.cloned.1.call-done) | copy-start | bytes 786436
  231.9 42.7 %copy-start.39 = (f32[64]{0:T(128)S(1)}, f32[64]{0:T(128)}, u32[]{:S(2)}) copy-start(f32[64]{0:T(128)} %copy-done.37) | copy-start | bytes 772
  231.9 42.7 %copy-start.48 = (f32[64]{0:T(128)S(1)}, f32[64]{0:T(128)}, u32[]{:S(2)}) copy-start(f32[64]{0:T(128)} %copy-done.47) | copy-start | bytes 772
  (14 other events, 13.4 us)
Sparse Core Ops, SparseCore 0:
  9.9 28.3 all-gather.3
  46.6 35.7 reduce-scatter.8
  84.4 37.8 all-gather.5
  124.2 29.3 all-gather.7
  161.2 27.1 reduce-scatter.12
  213.4 20.6 reduce-scatter.14
  236.4 19.9 reduce-scatter.10
  259.8 44.4 reduce-scatter.16
  308.1 76.4 reduce-scatter.20
  388.6 36.0 reduce-scatter.18
  429.0 53.8 reduce-scatter.22
where the time goes:
time: 490 us; the launch traced here: 489 us
  waiting for transfers between devices  297 us (61%)
  blocking collectives  121 us (25%)
  matrix products  31.5 us (6%)
  between operations  14.5 us (3%)
  other arithmetic  11.5 us (2%)
  local copies, waits for them, and re-layouts  10.4 us (2%)
    reduce_scatter x1, waiting for transfers between devices, shards(): lax.psum_scatter(gate_up_part, 'dp', scatter_dimension=1, tiled=True)  78.5 us
    reduce_scatter x1, waiting for transfers between devices, shards(): lax.psum_scatter(down_part, 'dp', scatter_dimension=1, tiled=True)  58.3 us
    psum x1, blocking collectives, shards(): lax.psum((first_part, second_part, kernel_full), ('dp', 'tensor'))  39.3 us
    reduce_scatter x1, waiting for transfers between devices, shards(): lax.psum_scatter(out_part, 'dp', scatter_dimension=1, tiled=True)  37.3 us
    reduce_scatter x1, waiting for transfers between devices, shards(): lax.psum_scatter(in_part, 'dp', scatter_dimension=1, tiled=True)  27.7 us
    all_gather x1, waiting for transfers between devices, shards(): lax.all_gather(down_weight, 'dp', axis=1, tiled=True)  27.4 us
    reduce_scatter x1, waiting for transfers between devices, shards(): lax.psum_scatter(hidden_back, 'tensor', scatter_dimension=0, tiled=True)  27.2 us
    all_gather x1, waiting for transfers between devices, shards(): lax.all_gather(gate_up_weight, 'dp', axis=1, tiled=True)  22.1 us
  transfers between devices with their start and end apart: 13, of which 10 were waited for; matrix products, arithmetic and copies ran while one was open for 7% of the time, Pallas kernels for 0%

commit v1 on v0

--- a/solution.py
+++ b/solution.py
@@ -175,7 +175,7 @@
         lax.psum_scatter(down_part, "dp", scatter_dimension=1, tiled=True),
     )
     first_gain_grad, second_gain_grad, conv_grad = lax.psum(
-        (first_part, second_part, kernel_full), ("dp", "tensor")
+        lax.psum((first_part, second_part, kernel_full), "tensor"), "dp"
     )
     return (
         output,

time: 490 us -> 490 us (level)
    psum x1 -> x2, blocking collectives: 39.3 us -> 39.5 us  [the longest x1 23.4 us: shards(): lax.psum(lax.psum((first_part, second_part, kernel_full), 'tensor'), 'dp')]
where the time goes in v1:
time: 490 us; the launch traced here: 489 us
  waiting for transfers between devices  297 us (61%)
  blocking collectives  122 us (25%)
  matrix products  31.5 us (6%)
  between operations  14.5 us (3%)
  other arithmetic  11.5 us (2%)
  local copies, waits for them, and re-layouts  10.4 us (2%)
    reduce_scatter x1, waiting for transfers between devices, shards(): lax.psum_scatter(gate_up_part, 'dp', scatter_dimension=1, tiled=True)  78.5 us
    reduce_scatter x1, waiting for transfers between devices, shards(): lax.psum_scatter(down_part, 'dp', scatter_dimension=1, tiled=True)  58.3 us
    reduce_scatter x1, waiting for transfers between devices, shards(): lax.psum_scatter(out_part, 'dp', scatter_dimension=1, tiled=True)  37.3 us
    reduce_scatter x1, waiting for transfers between devices, shards(): lax.psum_scatter(in_part, 'dp', scatter_dimension=1, tiled=True)  27.4 us
    all_gather x1, waiting for transfers between devices, shards(): lax.all_gather(down_weight, 'dp', axis=1, tiled=True)  27.4 us
    reduce_scatter x1, waiting for transfers between devices, shards(): lax.psum_scatter(hidden_back, 'tensor', scatter_dimension=0, tiled=True)  27.2 us
    psum x1, blocking collectives, shards(): lax.psum(lax.psum((first_part, second_part, kernel_full), 'tensor'), 'dp')  23.4 us
    all_gather x1, waiting for transfers between devices, shards(): lax.all_gather(gate_up_weight, 'dp', axis=1, tiled=True)  22.1 us
  transfers between devices with their start and end apart: 13, of which 10 were waited for; matrix products, arithmetic and copies ran while one was open for 7% of the time, Pallas kernels for 0%

profile of v1, /device:TPU:0, one launch (start us, length us, event | category | flops | bytes accessed | tf_op | source)
XLA Modules:
  0.0 489.5 jit_solution(7870595740377648362)
XLA Ops:
  7.2 0.7 all-gather.4.cloned.1.call-update
  8.0 0.8 reduce-window.8
  8.9 11.7 %all_gather.30 = bf16[256,1024]{1,0:T(8,128)(2,1)S(1)} all-gather(bf16[256,128]{1,0:T(8,128)(2,1)} %param.14), channel_id=1, replica_groups=mesh['dp'=8,'tensor'=4] {'dp'}, dimensions={1}, use_global_device_ids=true | all-gather | bytes 589824 | tf_op jit(solution)/shard_map/all_gather | solution.py:74
  20.6 1.1 fusion.18
  21.8 1.0 fusion.15
  22.8 16.4 %all_gather.28 = bf16[256,1024]{1,0:T(8,128)(2,1)S(1)} all-gather(bf16[64,1024]{1,0:T(8,128)(2,1)S(1)} %fusion.15), channel_id=1, replica_groups=mesh['dp'=8,'tensor'=4] {'tensor'}, dimensions={0}, use_global_device_ids=true | all-gather | bytes 655360 | tf_op jit(solution)/shard_map/all_gather | solution.py:69
  39.9 2.0 convolution_bitcast_fusion.5
  42.0 1.3 collective-permute-start
  43.3 0.9 fusion.34
  44.2 0.9 multiply_convert_fusion.8
  45.1 1.3 fusion.37
  46.5 0.7 all-gather.6.cloned.1.call-update
  47.8 21.5 %all_gather.34 = bf16[256,1024]{1,0:T(8,128)(2,1)} all-gather(bf16[64,1024]{1,0:T(8,128)(2,1)S(1)} %copy-done.13), channel_id=1, replica_groups=mesh['dp'=8,'tensor'=4] {'tensor'}, dimensions={0}, use_global_device_ids=true | all-gather | bytes 655360 | tf_op jit(solution)/shard_map/all_gather | solution.py:115
  69.3 13.1 %reduce-scatter.9.cloned.1.call-done = f32[64,1024]{1,0:T(8,128)} async-done(((f32[256,1024]{1,0:T(8,128)}), f32[64,1024]{1,0:T(8,128)}) %reduce-scatter.9.cloned.1.call-update) | async-done | bytes 262160 | tf_op jit(solution)/shard_map/reduce_scatter | solution.py:92
  82.4 1.1 multiply_reduce_fusion.5
  83.6 16.7 %all_gather.31 = bf16[256,1024]{1,0:T(8,128)(2,1)} all-gather(bf16[64,1024]{1,0:T(8,128)(2,1)S(1)} %multiply_convert_fusion.7), channel_id=1, replica_groups=mesh['dp'=8,'tensor'=4] {'tensor'}, dimensions={0}, use_global_device_ids=true | all-gather | bytes 655360 | tf_op jit(solution)/shard_map/all_gather | solution.py:93
  100.3 22.1 %all-gather.6.cloned.1.call-done = bf16[2,1024,1152]{2,1,0:T(8,128)(2,1)} async-done(((bf16[2,128,1152]{2,1,0:T(8,128)(2,1)}), bf16[2,1024,1152]{2,1,0:T(8,128)(2,1)}) %all-gather.6.cloned.1.call-update) | async-done | bytes 4718608 | tf_op jit(solution)/shard_map/all_gather | solution.py:75
  122.4 3.9 convolution_bitcast_fusion.1
  126.2 27.4 %all-gather.8.cloned.1.call-done = bf16[1152,1024]{1,0:T(8,128)(2,1)} async-done(((bf16[1152,128]{1,0:T(8,128)(2,1)}), bf16[1152,1024]{1,0:T(8,128)(2,1)}) %all-gather.8.cloned.1.call-update) | async-done | bytes 2359312 | tf_op jit(solution)/shard_map/all_gather | solution.py:76
  153.6 4.1 fusion.3
  157.7 0.8 copy-done.18
  158.7 2.4 convolution_bitcast_fusion.4
  161.2 27.2 %reduce-scatter.13.cloned.1.call-done = f32[64,1024]{1,0:T(8,128)} async-done(((f32[256,1024]{1,0:T(8,128)}), f32[64,1024]{1,0:T(8,128)}) %reduce-scatter.13.cloned.1.call-update) | async-done | bytes 262160 | tf_op jit(solution)/shard_map/reduce_scatter | solution.py:129
  188.4 1.2 multiply_reduce_fusion
  190.1 1.1 fusion.32
  191.3 15.9 %all_gather.35 = bf16[256,1024]{1,0:T(8,128)(2,1)S(1)} all-gather(bf16[64,1024]{1,0:T(8,128)(2,1)S(1)} %fusion.32), channel_id=1, replica_groups=mesh['dp'=8,'tensor'=4] {'tensor'}, dimensions={0}, use_global_device_ids=true | all-gather | bytes 655360 | tf_op jit(solution)/shard_map/all_gather | solution.py:132
  207.7 1.4 collective-permute-start.1
  209.1 1.7 collective-permute-done.1
  210.9 0.8 multiply_reduce_fusion.3
  211.8 1.4 fusion
  213.4 3.4 convolution_convert_fusion
  216.9 2.3 convolution_bitcast_fusion.2
  219.2 1.0 copy-done.3
  220.4 6.1 %convolution_bitcast_fusion = f32[2,1024,1152]{1,2,0:T(8,128)} fusion(bf16[1,256,1152]{2,1,0:T(8,128)(2,1)} %copy-done.20, bf16[1,256,1152]{2,1,0:T(8,128)(2,1)S(1)} %copy-done.19, bf16[256,1024]{1,0:T(8,128)(2,1)S(1)} %copy-done.3), kind=kOutput, calls=%fused_computation | convolution fusion | flops 1208549376 | bytes 11141120 | tf_op jit(solution)/shard_map/td,ktf->kdf/dot_general | solution.py:123
  226.6 0.8 copy-done.16
  227.4 1.3 fusion.39
  228.8 3.0 fusion.40
  232.6 1.5 reduce-scatter.15.cloned.1.call-done
  234.1 1.1 fusion.17
  235.3 16.2 %all-reduce.1 = (f32[1024]{0:T(1024)S(1)}, f32[3,1024]{1,0:T(4,128)S(1)}, f32[1024]{0:T(1024)S(1)}) all-reduce(f32[1024]{0:T(1024)S(1)} %get-tuple-element.32, f32[3,1024]{1,0:T(4,128)S(1)} %maximum_dynamic-update-slice_fusion, f32[1024]{0:T(1024)S(1)} %get-tuple-element.30), channel_id=1, replica_groups=mesh['dp'=8,'tensor'=4] {'tensor'}, use_global_device_ids=true, to_apply=%region_11.12 | all-reduce | flops 5120 | bytes 40960 | tf_op jit(solution)/shard_map/psum | solution.py:178
  251.4 23.4 %all-reduce = (f32[1024]{0:T(1024)}, f32[3,1024]{1,0:T(4,128)}, f32[1024]{0:T(1024)}) all-reduce(f32[1024]{0:T(1024)S(1)} %get-tuple-element.37, f32[3,1024]{1,0:T(4,128)S(1)} %get-tuple-element.38, f32[1024]{0:T(1024)S(1)} %get-tuple-element.39), channel_id=1, replica_groups=mesh['dp'=8,'tensor'=4] {'dp'}, use_global_device_ids=true, to_apply=%region_12.13 | all-reduce | flops 5120 | bytes 40960 | tf_op jit(solution)/shard_map/psum | solution.py:177
  274.8 1.9 fusion.14
  276.7 27.4 %reduce-scatter.17.cloned.1.call-done = f32[3,128,256]{1,2,0:T(8,128)} async-done(((f32[3,1024,256]{1,2,0:T(8,128)}), f32[3,128,256]{1,2,0:T(8,128)}) %reduce-scatter.17.cloned.1.call-update) | async-done | bytes 393232 | tf_op jit(solution)/shard_map/reduce_scatter | solution.py:172
  304.2 1.9 copy.25
  306.1 78.5 %reduce-scatter.21.cloned.1.call-done = f32[2,128,1152]{1,2,0:T(8,128)} async-done(((f32[2,1024,1152]{1,2,0:T(8,128)}), f32[2,128,1152]{1,2,0:T(8,128)}) %reduce-scatter.21.cloned.1.call-update) | async-done | bytes 1179664 | tf_op jit(solution)/shard_map/reduce_scatter | solution.py:174
  384.6 2.7 copy.26
  387.3 37.3 %reduce-scatter.19.cloned.1.call-done = f32[256,128]{1,0:T(8,128)} async-done(((f32[256,1024]{1,0:T(8,128)}), f32[256,128]{1,0:T(8,128)}) %reduce-scatter.19.cloned.1.call-update) | async-done | bytes 131088 | tf_op jit(solution)/shard_map/reduce_scatter | solution.py:173
  424.6 58.3 %reduce-scatter.23.cloned.1.call-done = f32[1152,128]{1,0:T(8,128)} async-done(((f32[1152,1024]{1,0:T(8,128)}), f32[1152,128]{1,0:T(8,128)}) %reduce-scatter.23.cloned.1.call-update) | async-done | bytes 589840 | tf_op jit(solution)/shard_map/reduce_scatter | solution.py:175
  (137 shorter events, 4.2 us)
Async XLA Ops:
  7.2 32.7 %all-gather.4.cloned.1.call-start = ((), (), s32[]{:S(2)}) async-start(), calls=%async_computation.8 | async-start | bytes 1769472 | tf_op jit(solution)/shard_map/all_gather | solution.py:73
  7.9 74.5 %reduce-scatter.9.cloned.1.call-start = ((), (), s32[]{:S(2)}) async-start(), calls=%async_computation.9 | async-start | bytes 1310720 | tf_op jit(solution)/shard_map/reduce_scatter | solution.py:92
  20.6 24.5 %copy-start.4 = (bf16[256,1024]{1,0:T(8,128)(2,1)}, bf16[256,1024]{1,0:T(8,128)(2,1)S(1)}, u32[]{:S(2)}) copy-start(bf16[256,1024]{1,0:T(8,128)(2,1)S(1)} %all_gather.30) | copy-start | bytes 1572868
  21.8 17.5 %copy-start.40 = (f32[64]{0:T(128)}, f32[64]{0:T(128)S(1)}, u32[]{:S(2)}) copy-start(f32[64]{0:T(128)S(1)} %add_rsqrt_fusion.1) | copy-start | bytes 772
  39.2 2.8 copy-start.6
  39.9 4.3 copy-start.33
  39.9 4.3 copy-start.35
  42.0 2.2 collective-permute-start
  45.1 2.1 copy-start.15
  45.1 2.7 copy-start.13
  46.4 36.0 %copy-start.8 = (bf16[64,1024]{1,0:T(8,128)(2,1)S(1)}, bf16[64,1024]{1,0:T(8,128)(2,1)}, u32[]{:S(2)}) copy-start(bf16[64,1024]{1,0:T(8,128)(2,1)} %param.10) | copy-start | bytes 393220
  46.4 37.1 %copy-start.25 = (f32[1024]{0:T(1024)S(1)}, f32[1024]{0:T(1024)}, u32[]{:S(2)}) copy-start(f32[1024]{0:T(1024)} %param.15) | copy-start | bytes 12292
  46.4 75.9 %all-gather.6.cloned.1.call-start = ((), (), s32[]{:S(2)}) async-start(), calls=%async_computation.10 | async-start | bytes 5308416 | tf_op jit(solution)/shard_map/all_gather | solution.py:75
  47.2 106.4 %all-gather.8.cloned.1.call-start = ((), (), s32[]{:S(2)}) async-start(), calls=%async_computation.11 | async-start | bytes 2654208 | tf_op jit(solution)/shard_map/all_gather | solution.py:76
  47.8 140.6 %reduce-scatter.13.cloned.1.call-start = ((), (), s32[]{:S(2)}) async-start(), calls=%async_computation.13 | async-start | bytes 1310720 | tf_op jit(solution)/shard_map/reduce_scatter | solution.py:129
  83.5 16.8 %copy-start.1 = (f32[64,1024]{1,0:T(8,128)}, f32[64,1024]{1,0:T(8,128)S(1)}, u32[]{:S(2)}) copy-start(f32[64,1024]{1,0:T(8,128)S(1)} %get-tuple-element.43) | copy-start | bytes 786436
  83.5 16.8 %copy-start.37 = (f32[64]{0:T(128)}, f32[64]{0:T(128)S(1)}, u32[]{:S(2)}) copy-start(f32[64]{0:T(128)S(1)} %add_rsqrt_fusion) | copy-start | bytes 772
  153.6 5.1 %copy-start = (bf16[2,1024,1152]{2,1,0:T(8,128)(2,1)S(1)}, bf16[2,1024,1152]{2,1,0:T(8,128)(2,1)}, u32[]{:S(2)}) copy-start(bf16[2,1024,1152]{2,1,0:T(8,128)(2,1)} %all-gather.6.cloned.1.call-done) | copy-start | bytes 14155780
  158.7 29.7 %copy-start.2 = (f32[64,1024]{1,0:T(8,128)S(1)}, f32[64,1024]{1,0:T(8,128)}, u32[]{:S(2)}) copy-start(f32[64,1024]{1,0:T(8,128)} %copy-done.1) | copy-start | bytes 786436
  158.7 29.7 %copy-start.38 = (f32[64]{0:T(128)S(1)}, f32[64]{0:T(128)}, u32[]{:S(2)}) copy-start(f32[64]{0:T(128)} %copy-done.37) | copy-start | bytes 772
  161.1 29.0 %copy-start.14 = (bf16[64,1024]{1,0:T(8,128)(2,1)S(1)}, bf16[64,1024]{1,0:T(8,128)(2,1)}, u32[]{:S(2)}) copy-start(bf16[64,1024]{1,0:T(8,128)(2,1)} %param.18) | copy-start | bytes 393220
  161.1 46.1 %copy-start.5 = (bf16[256,1024]{1,0:T(8,128)(2,1)S(1)}, bf16[256,1024]{1,0:T(8,128)(2,1)}, u32[]{:S(2)}) copy-start(bf16[256,1024]{1,0:T(8,128)(2,1)} %copy-done.4) | copy-start | bytes 1572868
  161.1 46.4 %copy-start.17 = (f32[256,256]{1,0:T(8,128)S(1)}, f32[256,256]{1,0:T(8,128)}, u32[]{:S(2)}) copy-start(f32[256,256]{1,0:T(8,128)} %get-tuple-element.45) | copy-start | bytes 786436
  161.1 73.0 %reduce-scatter.15.cloned.1.call-start = ((), (), s32[]{:S(2)}) async-start(), calls=%async_computation.14 | async-start | bytes 655360 | tf_op jit(solution)/shard_map/reduce_scatter | solution.py:166
  191.2 19.7 %copy-start.28 = (f32[1,256]{1,0:T(1,128)S(1)}, f32[1,256]{1,0:T(1,128)}, u32[]{:S(2)}) copy-start(f32[1,256]{1,0:T(1,128)} %copy-done.27) | copy-start | bytes 3076
  191.2 19.7 %copy-start.30 = (f32[1,256]{1,0:T(1,128)S(1)}, f32[1,256]{1,0:T(1,128)}, u32[]{:S(2)}) copy-start(f32[1,256]{1,0:T(1,128)} %copy-done.29) | copy-start | bytes 3076
  191.2 19.7 %copy-start.32 = (f32[1,256]{1,0:T(1,128)S(1)}, f32[1,256]{1,0:T(1,128)}, u32[]{:S(2)}) copy-start(f32[1,256]{1,0:T(1,128)} %copy-done.31) | copy-start | bytes 3076
  191.2 19.7 %copy-start.34 = (f32[256]{0:T(256)S(1)}, f32[256]{0:T(256)}, u32[]{:S(2)}) copy-start(f32[256]{0:T(256)} %copy-done.33) | copy-start | bytes 3076
  191.2 19.6 %copy-start.36 = (f32[256]{0:T(256)S(1)}, f32[256]{0:T(256)}, u32[]{:S(2)}) copy-start(f32[256]{0:T(256)} %copy-done.35) | copy-start | bytes 3076
  191.3 19.6 %copy-start.45 = (f32[256]{0:T(256)S(1)}, f32[256]{0:T(256)}, u32[]{:S(2)}) copy-start(f32[256]{0:T(256)} %get-tuple-element.60) | copy-start | bytes 3076
  191.3 19.6 %copy-start.46 = (f32[256]{0:T(256)S(1)}, f32[256]{0:T(256)}, u32[]{:S(2)}) copy-start(f32[256]{0:T(256)} %get-tuple-element.65) | copy-start | bytes 3076
  207.6 4.2 copy-start.23
  207.7 4.2 copy-start.11
  207.7 3.2 collective-permute-start.1
  213.3 61.5 %reduce-scatter.11.cloned.1.call-start = ((), (), s32[]{:S(2)}) async-start(), calls=%async_computation.12 | async-start | bytes 655360 | tf_op jit(solution)/shard_map/reduce_scatter | solution.py:105
  213.3 3.5 copy-start.7
  213.3 3.5 copy-start.22
  213.4 3.5 copy-start.24
  216.8 87.3 %reduce-scatter.17.cloned.1.call-start = ((), (), s32[]{:S(2)}) async-start(), calls=%async_computation.15 | async-start | bytes 3538944 | tf_op jit(solution)/shard_map/reduce_scatter | solution.py:172
  219.2 165.4 %reduce-scatter.21.cloned.1.call-start = ((), (), s32[]{:S(2)}) async-start(), calls=%async_computation.17 | async-start | bytes 10616832 | tf_op jit(solution)/shard_map/reduce_scatter | solution.py:174
  226.6 2.3 copy-start.10
  226.6 198.0 %reduce-scatter.19.cloned.1.call-start = ((), (), s32[]{:S(2)}) async-start(), calls=%async_computation.16 | async-start | bytes 1179648 | tf_op jit(solution)/shard_map/reduce_scatter | solution.py:173
  228.8 254.2 %reduce-scatter.23.cloned.1.call-start = ((), (), s32[]{:S(2)}) async-start(), calls=%async_computation.18 | async-start | bytes 5308416 | tf_op jit(solution)/shard_map/reduce_scatter | solution.py:175
  231.9 2.3 copy-start.26
  231.9 2.3 copy-start.41
  231.9 42.9 %copy-start.9 = (f32[64,1024]{1,0:T(8,128)S(1)}, f32[64,1024]{1,0:T(8,128)}, u32[]{:S(2)}) copy-start(f32[64,1024]{1,0:T(8,128)} %reduce-scatter.13.cloned.1.call-done) | copy-start | bytes 786436
  231.9 42.9 %copy-start.39 = (f32[64]{0:T(128)S(1)}, f32[64]{0:T(128)}, u32[]{:S(2)}) copy-start(f32[64]{0:T(128)} %copy-done.37) | copy-start | bytes 772
  231.9 42.9 %copy-start.48 = (f32[64]{0:T(128)S(1)}, f32[64]{0:T(128)}, u32[]{:S(2)}) copy-start(f32[64]{0:T(128)} %copy-done.47) | copy-start | bytes 772
  (14 other events, 13.4 us)
Sparse Core Ops, SparseCore 0:
  9.9 28.3 all-gather.3
  46.6 35.7 reduce-scatter.8
  84.4 37.8 all-gather.5
  124.2 29.3 all-gather.7
  161.2 27.1 reduce-scatter.12
  213.4 20.6 reduce-scatter.14
  236.4 19.9 reduce-scatter.10
  259.8 44.3 reduce-scatter.16
  308.1 76.4 reduce-scatter.20
  388.5 36.0 reduce-scatter.18
  429.0 53.8 reduce-scatter.22
